TPU v7x, 256 devices: a whole 4x4x8 slice. The times are simulated.
256 devices in a mesh: genome: 16 (over y_hi, z), track: 16 (over y_lo, x, core).
Axes of the slice: x: 4, y: 4 (y_hi: 2, y_lo: 2; y = y_hi * 2 + y_lo), z: 8, core: 2. Of those that a mesh axis runs over, the one named last changes fastest.
Arguments:
- counts: bfloat16 [10240, 98304], P('track', 'genome'), may hold values from 0.2 to 20
- avail: int32 [80, 192], P('track', 'genome'), may hold values from 0 to 1, as said below
- track_factors: float32 [10240, 64], P('track'), may hold values from 0.1 to 1
- bin_factors: float32 [64, 98304], P(None, 'genome'), may hold values from 0.1 to 1
Outputs:
- new_tracks: float32 [10240, 64], P('track')
- new_bins: float32 [64, 98304], P(None, 'genome')
Inputs may be any that keep to these rules, and one draw needn't show every extreme that they name: Every block row and every block column of avail holds a 1.
All inputs are finite; a program needn't handle non-finite values.
Results may differ from a plain program's by a relative error of at most 0.00043.
Values sent between devices are 32-bit elements; how exact they have to be, the bound alone decides.
A program may use at most 128 MiB of HBM per device.

v0:
```python
import jax
import jax.numpy as jnp
from jax import lax
from jax.sharding import PartitionSpec as P

ITERS = 2


def make_ratio(counts, keep4, w_low, h_low):
    recon = jnp.dot(w_low, h_low, preferred_element_type=jnp.float32)
    rows, cols = counts.shape
    shaped = (counts.astype(jnp.float32) / recon).reshape(rows // 128, 128, cols // 512, 512)
    return jnp.where(keep4, shaped, 0.0).reshape(rows, cols).astype(jnp.bfloat16)


def body(counts, avail, track_factors, bin_factors):
    rows, cols = counts.shape
    programs = track_factors.shape[1]
    tblocks = rows // 128
    bblocks = cols // 512
    keep4 = (avail > 0)[:, None, :, None]
    avail_float = avail.astype(jnp.float32)
    w_now = track_factors
    h_now = bin_factors
    for step in range(ITERS):
        w_low = w_now.astype(jnp.bfloat16)
        w_blocks = w_now.reshape(tblocks, 128, programs).sum(axis=1)
        den_local = jnp.dot(avail_float.T, w_blocks, precision=lax.Precision.HIGHEST)
        ratio = make_ratio(counts, keep4, w_low, h_now.astype(jnp.bfloat16))
        num_local = lax.dot_general(
            w_low, ratio, (((0,), (0,)), ((), ())), preferred_element_type=jnp.float32
        )
        num_bins, den_block = lax.psum((num_local, den_local), "track")
        den_full = jnp.repeat(den_block.T, 512, axis=1)
        h_now = h_now * num_bins / den_full
        h_low = h_now.astype(jnp.bfloat16)
        ratio = make_ratio(counts, keep4, w_low, h_low)
        num_rows = lax.dot_general(
            ratio, h_low, (((1,), (1,)), ((), ())), preferred_element_type=jnp.float32
        )
        h_blocks = h_now.reshape(programs, bblocks, 512).sum(axis=2)
        den_rows = jnp.dot(avail_float, h_blocks.T, precision=lax.Precision.HIGHEST)
        num_tracks, den_tracks = lax.psum((num_rows, den_rows), "genome")
        w_now = (
            w_now.reshape(tblocks, 128, programs)
            * num_tracks.reshape(tblocks, 128, programs)
            / den_tracks[:, None, :]
        ).reshape(rows, programs)
    return (w_now, h_now)


def solution(mesh):
    placed = (P("track", "genome"), P("track", "genome"), P("track", None), P(None, "genome"))
    return jax.shard_map(
        body,
        mesh=mesh,
        in_specs=placed,
        out_specs=(P("track", None), P(None, "genome")),
        check_vma=False,
    )
```

profile of v0, /device:TPU:2, one launch (start us, length us, event | category | flops | bytes accessed | tf_op | source)
XLA Modules:
  0.0 622.9 jit_solution(17060776115540105943)
XLA Ops:
  7.2 0.0 all-reduce.5.cloned.1.call-start
  7.2 0.7 broadcast_compare_fusion
  7.9 1.4 broadcast_in_dim.35
  9.3 0.0 copy-start
  9.4 9.9 %copy.20 = pred[80,8,12,512]{3,1,2,0:T(8,128)(4,1)} copy(pred[80,8,12,512]{3,2,1,0:T(8,128)(4,1)S(1)} %bitcast.35) | data formatting | bytes 7864320
  19.3 10.0 %fusion.14 = f32[64,6144]{1,0:T(8,128)} fusion(pred[640,6144]{1,0:T(8,128)(4,1)} %bitcast.40, bf16[640,6144]{1,0:T(8,128)(2,1)} %param.4, f32[64,6144]{1,0:T(8,128)S(1)} %copy-done, f32[640,64]{0,1:T(8,128)S(1)} %copy-done.1), kind=kOutput, calls=%fused_computation.15 | convolution fusion | flops 1022836736 | bytes 15106048 | tf_op jit(solution)/shard_map/dot_general | solution.py:30
  29.3 0.0 all-reduce.5.cloned.1.call-update
  29.3 0.0 all-reduce.7.cloned.1.call-start
  29.4 0.1 reduce_sum.36
  29.5 0.2 fusion.45
  29.7 27.0 %psum.57 = f32[64,12]{0,1:T(8,128)S(1)} all-reduce(f32[64,12]{0,1:T(8,128)S(1)} %fusion.45), channel_id=1, replica_groups=mesh['genome'=16,'track'=16] {'track'}, use_global_device_ids=true, to_apply=%region_2.3 | all-reduce | flops 768 | bytes 6144 | tf_op jit(solution)/shard_map/psum | solution.py:33
  56.7 0.1 copy.14
  56.8 0.2 broadcast_in_dim.38
  57.0 0.9 copy.21
  58.0 97.3 %all-reduce.5.cloned.1.call-done = f32[64,6144]{1,0:T(8,128)} async-done(((f32[64,6144]{1,0:T(8,128)}), f32[64,6144]{1,0:T(8,128)}) %all-reduce.5.cloned.1.call-update) | async-done | bytes 1572880 | tf_op jit(solution)/shard_map/psum | solution.py:33
  155.3 2.1 multiply_divide_fusion.1
  157.4 9.7 %fusion.23 = f32[640,64]{0,1:T(8,128)} fusion(pred[640,6144]{1,0:T(8,128)(4,1)} %bitcast.41, bf16[640,6144]{1,0:T(8,128)(2,1)} %param.4, f32[64,6144]{1,0:T(8,128)S(1)} %multiply_divide_fusion.1, f32[640,64]{0,1:T(8,128)} %param.6), kind=kOutput, calls=%fused_computation.19 | convolution fusion | flops 1023188992 | bytes 13697024 | tf_op jit(solution)/shard_map/dot_general | solution.py:38
  167.1 1.9 reshape.46
  169.0 0.0 all-reduce.7.cloned.1.call-update
  169.0 0.0 all-reduce.9.cloned.1.call-start
  169.0 1.8 reduce_sum.37
  170.9 0.1 convolution_bitcast_fusion.1
  171.0 42.3 %psum.59 = f32[5,64]{1,0:T(8,128)S(1)} all-reduce(f32[5,64]{1,0:T(8,128)S(1)} %convolution_bitcast_fusion.1), channel_id=1, replica_groups=mesh['genome'=16,'track'=16] {'genome'}, use_global_device_ids=true, to_apply=%region_5.6 | all-reduce | flops 320 | bytes 2560 | tf_op jit(solution)/shard_map/psum | solution.py:43
  213.3 0.1 copy.16
  213.4 105.7 %all-reduce.7.cloned.1.call-done = f32[640,64]{0,1:T(8,128)} async-done(((f32[640,64]{0,1:T(8,128)}), f32[640,64]{0,1:T(8,128)}) %all-reduce.7.cloned.1.call-update) | async-done | bytes 163856 | tf_op jit(solution)/shard_map/psum | solution.py:43
  319.1 0.1 div.46
  319.3 1.0 bitcast_divide_fusion.1
  320.2 9.8 %fusion.8 = f32[64,6144]{1,0:T(8,128)} fusion(pred[640,6144]{1,0:T(8,128)(4,1)} %bitcast.42, bf16[640,6144]{1,0:T(8,128)(2,1)} %param.4, f32[64,6144]{1,0:T(8,128)S(1)} %multiply_divide_fusion.1, f32[640,64]{0,1:T(8,128)S(1)} %bitcast_divide_fusion.1), kind=kOutput, calls=%fused_computation.12 | convolution fusion | flops 1022836736 | bytes 15106048 | tf_op jit(solution)/shard_map/dot_general | solution.py:30
  330.1 0.0 all-reduce.9.cloned.1.call-update
  330.1 0.0 all-reduce.11.cloned.1.call-start
  330.2 0.2 fusion.32
  330.4 0.2 fusion.42
  330.6 23.8 %psum.61 = f32[64,12]{0,1:T(8,128)S(1)} all-reduce(f32[64,12]{0,1:T(8,128)S(1)} %fusion.42), channel_id=1, replica_groups=mesh['genome'=16,'track'=16] {'track'}, use_global_device_ids=true, to_apply=%region_8.9 | all-reduce | flops 768 | bytes 6144 | tf_op jit(solution)/shard_map/psum | solution.py:33
  354.5 0.1 copy.17
  354.6 0.2 broadcast_in_dim.39
  354.8 0.9 copy.23
  355.7 93.6 %all-reduce.9.cloned.1.call-done = f32[64,6144]{1,0:T(8,128)} async-done(((f32[64,6144]{1,0:T(8,128)}), f32[64,6144]{1,0:T(8,128)}) %all-reduce.9.cloned.1.call-update) | async-done | bytes 1572880 | tf_op jit(solution)/shard_map/psum | solution.py:33
  449.3 2.8 multiply_divide_fusion
  452.1 1.7 reshape.49
  453.8 10.5 %fusion.12 = f32[640,64]{0,1:T(8,128)} fusion(pred[640,6144]{1,0:T(8,128)(4,1)} %bitcast.43, bf16[640,6144]{1,0:T(8,128)(2,1)} %param.4, f32[64,6144]{1,0:T(8,128)} %multiply_divide_fusion, f32[640,64]{0,1:T(8,128)} %copy-done.4), kind=kOutput, calls=%fused_computation.14 | convolution fusion | flops 1023188992 | bytes 13697024 | tf_op jit(solution)/shard_map/dot_general | solution.py:38
  464.4 0.2 reduce_sum.39
  464.6 0.0 all-reduce.11.cloned.1.call-update
  464.6 0.1 convolution_bitcast_fusion
  464.8 42.2 %psum.63 = f32[5,64]{1,0:T(8,128)S(1)} all-reduce(f32[5,64]{1,0:T(8,128)S(1)} %convolution_bitcast_fusion), channel_id=1, replica_groups=mesh['genome'=16,'track'=16] {'genome'}, use_global_device_ids=true, to_apply=%region_11.12 | all-reduce | flops 320 | bytes 2560 | tf_op jit(solution)/shard_map/psum | solution.py:43
  506.9 0.1 copy.18
  507.0 107.5 %all-reduce.11.cloned.1.call-done = f32[640,64]{0,1:T(8,128)} async-done(((f32[640,64]{0,1:T(8,128)}), f32[640,64]{0,1:T(8,128)}) %all-reduce.11.cloned.1.call-update) | async-done | bytes 163856 | tf_op jit(solution)/shard_map/psum | solution.py:43
  614.6 0.1 div.53
  614.7 1.6 bitcast_divide_fusion
  (15 shorter events, 0.1 us)
Async XLA Ops:
  7.2 148.1 %all-reduce.5.cloned.1.call-start = ((), (), s32[]{:S(2)}) async-start(), calls=%async_computation | async-start | bytes 3145728 | tf_op jit(solution)/shard_map/psum | solution.py:33
  9.3 10.0 %copy-start = (f32[64,6144]{1,0:T(8,128)S(1)}, f32[64,6144]{1,0:T(8,128)}, u32[]{:S(2)}) copy-start(f32[64,6144]{1,0:T(8,128)} %param.7) | copy-start | bytes 4718596
  9.3 9.9 %copy-start.1 = (f32[640,64]{0,1:T(8,128)S(1)}, f32[640,64]{0,1:T(8,128)}, u32[]{:S(2)}) copy-start(f32[640,64]{0,1:T(8,128)} %param.6) | copy-start | bytes 491524
  19.3 10.2 %copy-start.6 = (s32[5,12]{1,0:T(8,128)S(1)}, s32[5,12]{1,0:T(8,128)}, u32[]{:S(2)}) copy-start(s32[5,12]{1,0:T(8,128)} %param.5) | copy-start | bytes 724
  29.3 289.8 %all-reduce.7.cloned.1.call-start = ((), (), s32[]{:S(2)}) async-start(), calls=%async_computation.1 | async-start | bytes 327680 | tf_op jit(solution)/shard_map/psum | solution.py:43
  167.1 152.1 %copy-start.2 = (f32[640,64]{0,1:T(8,128)S(1)}, f32[640,64]{0,1:T(8,128)}, u32[]{:S(2)}) copy-start(f32[640,64]{0,1:T(8,128)} %param.6) | copy-start | bytes 491524
  169.0 280.3 %all-reduce.9.cloned.1.call-start = ((), (), s32[]{:S(2)}) async-start(), calls=%async_computation.2 | async-start | bytes 3145728 | tf_op jit(solution)/shard_map/psum | solution.py:33
  320.2 9.9 %copy-start.4 = (f32[640,64]{0,1:T(8,128)}, f32[640,64]{0,1:T(8,128)S(1)}, u32[]{:S(2)}) copy-start(f32[640,64]{0,1:T(8,128)S(1)} %bitcast_divide_fusion.1) | copy-start | bytes 491524
  320.2 9.9 %copy-start.3 = (f32[640,64]{0,1:T(8,128)S(1)}, f32[640,64]{0,1:T(8,128)}, u32[]{:S(2)}) copy-start(f32[640,64]{0,1:T(8,128)} %all-reduce.7.cloned.1.call-done) | copy-start | bytes 491524
  330.1 284.5 %all-reduce.11.cloned.1.call-start = ((), (), s32[]{:S(2)}) async-start(), calls=%async_computation.3 | async-start | bytes 327680 | tf_op jit(solution)/shard_map/psum | solution.py:43
  453.8 160.9 %copy-start.5 = (f32[640,64]{0,1:T(8,128)S(1)}, f32[640,64]{0,1:T(8,128)}, u32[]{:S(2)}) copy-start(f32[640,64]{0,1:T(8,128)} %copy-done.4) | copy-start | bytes 491524
Sparse Core Ops, SparseCore 0:
  29.4 125.8 all-reduce.4
  169.1 149.9 all-reduce.6
  330.2 119.0 all-reduce.8
  464.7 149.7 all-reduce.10
where the time goes:
time: 623 us
  waiting for transfers between devices  404 us (65%)
  blocking collectives  135 us (22%)
  matrix products  40.8 us (7%)
  local copies, waits for them, and re-layouts  17.9 us (3%)
  between operations  14 us (2%)
  other arithmetic  10.5 us (2%)
    psum x2, waiting for transfers between devices, body(): num_tracks, den_tracks = lax.psum((num_rows, den_rows), 'genome')  213 us
    psum x2, waiting for transfers between devices, body(): num_bins, den_block = lax.psum((num_local, den_local), 'track')  191 us
    psum x2, blocking collectives, body(): num_tracks, den_tracks = lax.psum((num_rows, den_rows), 'genome')  84.5 us
    psum x2, blocking collectives, body(): num_bins, den_block = lax.psum((num_local, den_local), 'track')  50.8 us
    dot_general x2, matrix products, body(): lax.dot_general(ratio, h_low, (((1,), (1,)), ((), ())), preferred_element...  20.3 us
    dot_general x2, matrix products, body(): lax.dot_general(w_low, ratio, (((0,), (0,)), ((), ())), preferred_element...  19.8 us
  transfers between devices with their start and end apart: 4, of which 4 were waited for; matrix products, arithmetic and copies ran while one was open for 1% of the time, Pallas kernels for 0%

commit v1 on v0

v1 whole, which is shorter than its diff:
```python
import functools

import jax
import jax.numpy as jnp
from jax import lax
from jax.experimental import pallas as pl
from jax.experimental.pallas import tpu as pltpu
from jax.sharding import PartitionSpec as P

ITERS = 2
K = 64
ROWS = 640
COLS = 6144
TB = 128
BB = 512
NT = ROWS // TB
NB = COLS // BB
NC = NB // 2
HALF = 320
WIDE = 384
LAG = 3
GROUPS = ((0, 256), (256, 256), (512, 128))
MESH = pl.DeviceIdType.MESH
F32 = jnp.float32
BF16 = jnp.bfloat16


def kernel(
    counts, avail, w_in, h_in, w_out, h_out,
    cbuf, hbuf, wth, wrow, wcol, snd, own, crecv, rrecv, dsnd, dcrecv, drecv, dtot,
    acc, dacc, gsnd, grecv,
    csem, hsem, osem, cs, cr, rs, rr, gs, gr, fs, fr, ds_s, ds_r, ws, wr, us, ur,
):
    g = lax.axis_index("genome")
    t = lax.axis_index("track")
    yh, z = g // 8, g % 8
    p, c = t // 2, t % 2
    y, x = p // 4, p % 4
    sib = (g, p * 2 + (1 - c))

    def tpeer(d):
        q = ((y + d // 4) % 2) * 4 + (x + d % 4) % 4
        return q, (g, q * 2 + c)

    def gpeer(d):
        qh, qz = (yh + d // 8) % 2, (z + d % 8) % 8
        return qh, qz, (qh * 8 + qz, t)

    bar = pltpu.get_barrier_semaphore()
    pl.semaphore_signal(bar, inc=1, device_id=sib, device_id_type=MESH)
    for d in range(1, 8):
        pl.semaphore_signal(bar, inc=1, device_id=tpeer(d)[1], device_id_type=MESH)
    for d in range(1, 16):
        pl.semaphore_signal(bar, inc=1, device_id=gpeer(d)[2], device_id_type=MESH)

    def cols(b):
        return pl.ds(pl.multiple_of(b * BB, BB), BB)

    def count_copy(b):
        return pltpu.make_async_copy(counts.at[:, cols(b)], cbuf.at[:, cols(b)], csem.at[b])

    def h_copy(b):
        return pltpu.make_async_copy(h_in.at[:, cols(b)], hbuf.at[0, b], hsem.at[b])

    def out_copy(b):
        return pltpu.make_async_copy(hbuf.at[ITERS, b], h_out.at[:, cols(b)], osem.at[b])

    def start_in(j, _):
        for b in (2 * j + 1 - c, 2 * j + c):
            h_copy(b).start()
            count_copy(b).start()
        return 0

    lax.fori_loop(0, NC, start_in, 0)

    def remote(src, dst, s, r, dev):
        return pltpu.make_async_remote_copy(
            src_ref=src, dst_ref=dst, send_sem=s, recv_sem=r, device_id=dev, device_id_type=MESH
        )

    rows_p = pl.ds(pl.multiple_of(p * 8, 8), 8)
    rows_z = pl.ds(pl.multiple_of(z * 8, 8), 8)

    def core_copy(it, j):
        return remote(snd.at[it, j], crecv.at[it, j], cs.at[it, j], cr.at[it, j], sib)

    def reduce_copy(it, j, d):
        q, dev = tpeer(d)
        rows = pl.ds(pl.multiple_of(q * 8, 8), 8)
        return remote(own.at[it, j, rows], rrecv.at[it, j, d - 1], rs.at[it, j, d - 1], rr.at[it, j, d - 1], dev)

    def gather_copy(it, j, d):
        dev = tpeer(d)[1]
        ref = hbuf.at[it + 1, 2 * j + c, rows_p]
        return remote(ref, ref, gs.at[it, j, d - 1], gr.at[it, j, d - 1], dev)

    def forward_copy(it, j, which):
        ref = hbuf.at[it + 1, 2 * j + which]
        return remote(ref, ref, fs.at[it, j], fr.at[it, j], sib)

    def den_core(it):
        return remote(dsnd.at[it], dcrecv.at[it], ds_s.at[it, 0], ds_r.at[it, 0], sib)

    def den_copy(it, d):
        q, dev = tpeer(d)
        rows = pl.ds(pl.multiple_of(q * 8, 8), 8)
        return remote(dsnd.at[it + ITERS, rows], drecv.at[it, d - 1], ds_s.at[it, d], ds_r.at[it, d], dev)

    def track_copy(it, d):
        qh, qz, dev = gpeer(d)
        rows = pl.ds(pl.multiple_of(qz * 8, 8), 8)
        return remote(gsnd.at[it, qh, rows], grecv.at[it, d - 1], ws.at[it, d - 1], wr.at[it, d - 1], dev)

    def w_copy(it, d):
        dev = gpeer(d)[2]
        ref = wth.at[it + 1, yh, rows_z]
        return remote(ref, ref, us.at[it, d - 1], ur.at[it, d - 1], dev)

    lane = lax.broadcasted_iota(jnp.int32, (8, 128), 1)
    lane64 = lax.broadcasted_iota(jnp.int32, (K, 128), 1)

    def mask_of(tb, b):
        return avail[tb, b].astype(F32)

    def ratio_of(b, lo, n, h_low):
        recon = jnp.dot(wrow[lo : lo + n, :], h_low, preferred_element_type=F32)
        return (cbuf[lo : lo + n, cols(b)].astype(F32) / recon).astype(BF16)

    def bins_block(it, b):
        h_low = hbuf[it, b].astype(BF16)
        total = None
        for lo, n in GROUPS:
            ratio = ratio_of(b, lo, n, h_low)
            parts = [
                wcol[:, s : s + TB] * mask_of(s // TB, b) for s in range(lo, lo + n, TB)
            ]
            left = jnp.concatenate(parts, axis=1).astype(BF16)
            term = jnp.dot(left, ratio, preferred_element_type=F32)
            total = term if total is None else total + term
        return total

    def tracks_block(it, b):
        h_now = hbuf[it + 1, b]
        h_low = h_now.astype(BF16)
        h_sum = jnp.sum(h_now, axis=1, keepdims=True)
        keep = jnp.zeros((8, 128), F32)
        for tb in range(NT):
            keep = jnp.where(lane == 64 + tb, mask_of(tb, b), keep)
        dacc[...] += h_sum * keep[0:1, :]
        for lo, n in GROUPS:
            ratio = ratio_of(b, lo, n, h_low)
            term = lax.dot_general(h_low, ratio, (((1,), (1,)), ((), ())), preferred_element_type=F32)
            for s in range(lo, lo + n, TB):
                acc[:, s : s + TB] += term[:, s - lo : s - lo + TB] * mask_of(s // TB, b)

    def spread_w(wt):
        wcol[...] = wt.astype(BF16).astype(F32)

    w0 = w_in[...]
    wt0 = w0.T
    wrow[...] = w0.astype(BF16)
    spread_w(wt0)
    zero64 = jnp.zeros((K, 64), F32)
    wth[0, 0] = jnp.concatenate([wt0[:, :HALF], zero64], axis=1)
    wth[0, 1] = pltpu.roll(wt0[:, 256:640], HALF, 1)

    def w_full(it):
        left = wth[it, 0]
        right = pltpu.roll(wth[it, 1], 64, 1)
        mid = jnp.where(lane64 < 64, left[:, 256:384], right[:, 0:128])
        return jnp.concatenate([left[:, 0:256], mid, right[:, 128:384]], axis=1)

    def iteration(it, _):
        wt = w_full(it)
        den = jnp.zeros((K, 128), F32)
        for tb in range(NT):
            row = jnp.zeros((8, 128), F32)
            for b in range(NB):
                row = jnp.where(lane == b, mask_of(tb, b), row)
            w_sum = jnp.sum(wt[:, tb * TB : (tb + 1) * TB], axis=1, keepdims=True)
            den = den + w_sum * row[0:1, :]
        dsnd[it] = den

        @pl.when(it == 0)
        def _():
            pl.semaphore_wait(bar, 23)

        den_core(it).start()

        def stage_b(j):
            @pl.when(j == 0)
            def _():
                den_core(it).wait_recv()
                dsnd[it + ITERS] = dsnd[it] + dcrecv[it]
                for d in range(1, 8):
                    den_copy(it, d).start()

            core_copy(it, j).wait_recv()
            own[it, j] = own[it, j] + crecv[it, j]
            for d in range(1, 8):
                reduce_copy(it, j, d).start()

        def first(j, _):
            @pl.when(it == 0)
            def _():
                for b in (2 * j + 1 - c, 2 * j + c):
                    h_copy(b).wait()
                    count_copy(b).wait()

            snd[it, j] = bins_block(it, 2 * j + 1 - c)
            core_copy(it, j).start()

            @pl.when(j > 0)
            def _():
                stage_b(j - 1)

            own[it, j] = bins_block(it, 2 * j + c)
            return 0

        lax.fori_loop(0, NC, first, 0)
        stage_b(NC - 1)

        acc[...] = jnp.zeros((K, ROWS), F32)
        dacc[...] = jnp.zeros((K, 128), F32)

        def stage_c(j):
            @pl.when(j == 0)
            def _():
                tot = dsnd[it + ITERS, rows_p]
                for d in range(1, 8):
                    den_copy(it, d).wait_recv()
                    tot = tot + drecv[it, d - 1]
                dtot[...] = tot

            tot = own[it, j, rows_p]
            for d in range(1, 8):
                reduce_copy(it, j, d).wait_recv()
                tot = tot + rrecv[it, j, d - 1]
            b = 2 * j + c
            den = jnp.sum(jnp.where(lane == b, dtot[...], 0.0), axis=1, keepdims=True)
            hbuf[it + 1, b, rows_p] = hbuf[it, b, rows_p] * tot / den
            for d in range(1, 8):
                gather_copy(it, j, d).start()

        def stage_d(j):
            for d in range(1, 8):
                gather_copy(it, j, d).wait_recv()
            forward_copy(it, j, c).start()

        def stage_e(j):
            tracks_block(it, 2 * j + c)
            forward_copy(it, j, 1 - c).wait_recv()
            tracks_block(it, 2 * j + 1 - c)

            @pl.when(it == ITERS - 1)
            def _():
                out_copy(2 * j + c).start()
                out_copy(2 * j + 1 - c).start()

        def second(k, _):
            @pl.when(k < NC)
            def _():
                stage_c(k)

            @pl.when((k >= LAG) & (k < NC + LAG))
            def _():
                stage_d(k - LAG)

            @pl.when(k >= LAG + 1)
            def _():
                stage_e(k - LAG - 1)

            return 0

        lax.fori_loop(0, NC + LAG + 1, second, 0)

        full = acc[...]
        dvec = dacc[...]
        gsnd[it, 0, :, 0:256] = full[:, 0:256]
        gsnd[it, 0, :, 256:384] = jnp.where(lane64 < 64, full[:, 256:384], dvec)
        right = pltpu.roll(full[:, 256:640], HALF, 1)
        gsnd[it, 1, :, 0:256] = right[:, 0:256]
        gsnd[it, 1, :, 256:384] = jnp.where(lane64 < 64, right[:, 256:384], dvec)
        for d in range(1, 16):
            track_copy(it, d).start()
        tot = gsnd[it, yh, rows_z]
        for d in range(1, 16):
            track_copy(it, d).wait_recv()
            tot = tot + grecv[it, d - 1]
        wide = lax.broadcasted_iota(jnp.int32, (8, WIDE), 1)
        block = (wide + yh * HALF) // TB
        den = jnp.ones((8, WIDE), F32)
        for tb in range(NT):
            den = jnp.where(block == tb, tot[:, HALF + tb : HALF + tb + 1], den)
        wth[it + 1, yh, rows_z] = wth[it, yh, rows_z] * tot / den
        for d in range(1, 16):
            w_copy(it, d).start()
        for d in range(1, 16):
            w_copy(it, d).wait_recv()
        wt = w_full(it + 1)
        spread_w(wt)
        w_new = wt.T
        wrow[...] = w_new.astype(BF16)
        w_out[...] = w_new

        den_core(it).wait_send()
        for d in range(1, 8):
            den_copy(it, d).wait_send()
        for d in range(1, 16):
            track_copy(it, d).wait_send()
            w_copy(it, d).wait_send()

        def drain(j, _):
            core_copy(it, j).wait_send()
            forward_copy(it, j, c).wait_send()
            for d in range(1, 8):
                reduce_copy(it, j, d).wait_send()
                gather_copy(it, j, d).wait_send()
            return 0

        lax.fori_loop(0, NC, drain, 0)
        return 0

    lax.fori_loop(0, ITERS, iteration, 0)

    def finish(b, _):
        out_copy(b).wait()
        return 0

    lax.fori_loop(0, NB, finish, 0)


def body(counts, avail, track_factors, bin_factors):
    dma = pltpu.SemaphoreType.DMA
    vmem = pltpu.VMEM
    return pl.pallas_call(
        kernel,
        name="factorize",
        out_shape=(
            jax.ShapeDtypeStruct((ROWS, K), F32),
            jax.ShapeDtypeStruct((K, COLS), F32),
        ),
        in_specs=[
            pl.BlockSpec(memory_space=pl.ANY),
            pl.BlockSpec(memory_space=pltpu.SMEM),
            pl.BlockSpec(memory_space=pltpu.VMEM),
            pl.BlockSpec(memory_space=pl.ANY),
        ],
        out_specs=(
            pl.BlockSpec(memory_space=pltpu.VMEM),
            pl.BlockSpec(memory_space=pl.ANY),
        ),
        scratch_shapes=[
            vmem((ROWS, COLS), BF16),
            vmem((ITERS + 1, NB, K, BB), F32),
            vmem((ITERS + 1, 2, K, WIDE), F32),
            vmem((ROWS, K), BF16),
            vmem((K, ROWS), F32),
            vmem((ITERS, NC, K, BB), F32),
            vmem((ITERS, NC, K, BB), F32),
            vmem((ITERS, NC, K, BB), F32),
            vmem((ITERS, NC, 7, 8, BB), F32),
            vmem((2 * ITERS, K, 128), F32),
            vmem((ITERS, K, 128), F32),
            vmem((ITERS, 7, 8, 128), F32),
            vmem((8, 128), F32),
            vmem((K, ROWS), F32),
            vmem((K, 128), F32),
            vmem((ITERS, 2, K, WIDE), F32),
            vmem((ITERS, 15, 8, WIDE), F32),
            dma((NB,)), dma((NB,)), dma((NB,)),
            dma((ITERS, NC)), dma((ITERS, NC)),
            dma((ITERS, NC, 7)), dma((ITERS, NC, 7)),
            dma((ITERS, NC, 7)), dma((ITERS, NC, 7)),
            dma((ITERS, NC)), dma((ITERS, NC)),
            dma((ITERS, 8)), dma((ITERS, 8)),
            dma((ITERS, 15)), dma((ITERS, 15)),
            dma((ITERS, 15)), dma((ITERS, 15)),
        ],
        compiler_params=pltpu.CompilerParams(
            collective_id=0, has_side_effects=True, vmem_limit_bytes=56 * 1024 * 1024
        ),
    )(counts, avail, track_factors, bin_factors)


def solution(mesh):
    placed = (P("track", "genome"), P("track", "genome"), P("track", None), P(None, "genome"))
    return jax.shard_map(
        body,
        mesh=mesh,
        in_specs=placed,
        out_specs=(P("track", None), P(None, "genome")),
        check_vma=False,
    )
```

time: 623 us -> 111 us (0.18)
  waiting for transfers between devices: 404 us -> 0 us
  blocking collectives: 135 us -> 0 us
  Pallas kernels: 0 us -> 103 us
  matrix products: 40.8 us -> 0 us
  between operations: 14 us -> 0.64 us
  local copies, waits for them, and re-layouts: 17.9 us -> 6.26 us
  other arithmetic: 10.5 us -> 0 us
    psum x4 -> x0, waiting for transfers between devices: 404 us -> none  [the longest x2 213 us: body(): num_tracks, den_tracks = lax.psum((num_rows, den_rows), 'genome')]
    psum x4 -> x0, blocking collectives: 135 us -> none  [the longest x2 84.5 us: body(): num_tracks, den_tracks = lax.psum((num_rows, den_rows), 'genome')]
    pallas_call x0 -> x1, Pallas kernels: none -> 103 us  [body(): pl.pallas_call(kernel, name='factorize', out_shape=(jax.ShapeDtypeStruct(...]
    dot_general x8 -> x0, matrix products: 40.8 us -> none  [the longest x2 20.3 us: body(): lax.dot_general(ratio, h_low, (((1,), (1,)), ((), ())), preferred_element...]
    div x4 -> x0, other arithmetic: 7.47 us -> none  [the longest x2 4.87 us: body(): h_now = h_now * num_bins / den_full]
    unnamed x17 -> x2, local copies, waits for them, and re-layouts: 11.8 us -> 4.47 us
  transfers between devices with their start and end apart: 4 -> 0, of which waited for: 4 -> 0; matrix products, arithmetic and copies ran while one was open for 1% -> 0% of each run, Pallas kernels for 0% -> 0%
where the time goes in v1:
time: 111 us; the launch traced here: 110 us
  Pallas kernels  103 us (93%)
  local copies, waits for them, and re-layouts  6.26 us (6%)
    pallas_call x1, Pallas kernels, body(): pl.pallas_call(kernel, name='factorize', out_shape=(jax.ShapeDtypeStruct(...  103 us
    unnamed x2, local copies, waits for them, and re-layouts  4.47 us

profile of v1, /device:TPU:2, one launch (start us, length us, event | category | flops | bytes accessed | tf_op | source)
XLA Modules:
  0.0 110.1 jit_solution(6703413826724227722)
XLA Ops:
  0.6 1.8 %copy.6.w_in = f32[640,64]{1,0:T(8,128)} copy(f32[640,64]{0,1:T(8,128)} %param.6) | data formatting | bytes 327680 | tf_op args[2]
  2.4 103.2 %factorize.1 = (f32[640,64]{1,0:T(8,128)}, f32[64,6144]{1,0:T(8,128)}) custom-call(bf16[640,6144]{1,0:T(8,128)(2,1)} %counts.1, s32[5,12]{1,0:T(8,128)} %avail.1, f32[640,64]{1,0:T(8,128)} %copy.6.w_in, f32[64,6144]{1,0:T(8,128)} %h_in.1), custom_call_target="tpu_custom_call" | custom-call | tf_op jit(solution)/shard_map/factorize/pallas_call | solution.py:336
  105.7 1.8 %copy.7 = f32[640,64]{0,1:T(8,128)} copy(f32[640,64]{1,0:T(8,128)} %get-tuple-element.2) | data formatting | bytes 327680 | tf_op jit(solution)/shard_map/factorize/pallas_call | solution.py:336
  107.4 2.7 %copy.9 = f32[64,6144]{1,0:T(8,128)} copy(f32[64,6144]{1,0:T(8,128)} %get-tuple-element.7) | data formatting | bytes 3145728

commit v2 on v0

v2 whole, which is shorter than its diff:
```python
import jax
import jax.numpy as jnp
from jax import lax
from jax.experimental import pallas as pl
from jax.experimental.pallas import tpu as pltpu
from jax.sharding import PartitionSpec as P

ITERS = 2
K = 64
ROWS = 640
COLS = 6144
TB = 128
BB = 512
NT = ROWS // TB
NB = COLS // BB
NC = NB // 2
HALF = 320
WIDE = 384
LAG = 6
FAR = (12, 11, 13, 4, 10, 14, 3, 5, 9, 15, 2, 6, 8, 1, 7)
NEAR = (6, 2, 5, 1, 7, 3, 4)
TILES = (2, 0, 1)
CB = 2 * BB
MESH = pl.DeviceIdType.MESH
F32 = jnp.float32
BF16 = jnp.bfloat16


def kernel(
    counts, avail_in, w_in, h_in, w_out, h_out,
    avail, wbuf, cbuf, hbuf, wth, wrow, wcol, part, crecv, rrecv, dsnd, dcrecv, drecv, dtot,
    acc, dacc, gsnd, grecv,
    csem, hsem, osem, wsem, send, cr, rr, gr, fr, dr, wr,
):
    g = lax.axis_index("genome")
    t = lax.axis_index("track")
    yh, z = g // 8, g % 8
    p, c = t // 2, t % 2
    y, x = p // 4, p % 4
    sib = (g, p * 2 + (1 - c))

    def tpeer(d):
        q = ((y + d // 4) % 2) * 4 + (x + d % 4) % 4
        return q, (g, q * 2 + c)

    def gpeer(d):
        qh, qz = (yh + d // 8) % 2, (z + d % 8) % 8
        return qh, qz, (qh * 8 + qz, t)

    def cols(j):
        return pl.ds(pl.multiple_of(j * CB, CB), CB)

    def half(which):
        return pl.ds(pl.multiple_of(which * BB, BB), BB)

    def count_copy(j):
        return pltpu.make_async_copy(counts.at[:, cols(j)], cbuf.at[:, cols(j)], csem.at[j])

    def h_copy(j):
        return pltpu.make_async_copy(h_in.at[:, cols(j)], hbuf.at[0, j], hsem.at[j])

    def out_copy(j):
        return pltpu.make_async_copy(hbuf.at[ITERS, j], h_out.at[:, cols(j)], osem.at[j])

    def start_in(j, _):
        h_copy(j).start()
        count_copy(j).start()
        return 0

    w_copy_in = pltpu.make_async_copy(w_in, wbuf, wsem.at[0])
    w_copy_out = pltpu.make_async_copy(wbuf, w_out, wsem.at[1])
    w_copy_in.start()
    avail_copy = pltpu.make_async_copy(avail_in, avail, wsem.at[2])
    avail_copy.start()
    start_in(0, 0)

    bar = pltpu.get_barrier_semaphore()
    for d in FAR:
        pl.semaphore_signal(bar, inc=1, device_id=gpeer(d)[2], device_id_type=MESH)
    for d in range(1, 8):
        pl.semaphore_signal(bar, inc=1, device_id=tpeer(d)[1], device_id_type=MESH)
    pl.semaphore_signal(bar, inc=1, device_id=sib, device_id_type=MESH)

    def remote(src, dst, s, r, dev):
        return pltpu.make_async_remote_copy(
            src_ref=src, dst_ref=dst, send_sem=s, recv_sem=r, device_id=dev, device_id_type=MESH
        )

    rows_p = pl.ds(pl.multiple_of(p * 8, 8), 8)
    rows_z = pl.ds(pl.multiple_of(z * 8, 8), 8)

    def core_copy(it, j):
        return remote(part.at[it, j, :, half(1 - c)], crecv.at[it, j], send.at[0], cr.at[it, j], sib)

    def reduce_copy(it, j, d):
        q, dev = tpeer(d)
        rows = pl.ds(pl.multiple_of(q * 8, 8), 8)
        return remote(part.at[it, j, rows, half(c)], rrecv.at[it, j, d - 1], send.at[1], rr.at[it, j], dev)

    def reduce_all(it, j):
        return remote(rrecv.at[it, j], rrecv.at[it, j], send.at[1], rr.at[it, j], sib)

    def gather_copy(it, j, d):
        ref = hbuf.at[it + 1, j, rows_p, half(c)]
        return remote(ref, ref, send.at[2], gr.at[it, j], tpeer(d)[1])

    def gather_all(it, j):
        return remote(rrecv.at[it, j], rrecv.at[it, j], send.at[2], gr.at[it, j], sib)

    def forward_copy(it, j, which):
        ref = hbuf.at[it + 1, j, :, half(which)]
        return remote(ref, ref, send.at[3], fr.at[it, j], sib)

    def den_core(it):
        return remote(dsnd.at[it], dcrecv.at[it], send.at[4], dr.at[it, 0], sib)

    def den_copy(it, d):
        q, dev = tpeer(d)
        rows = pl.ds(pl.multiple_of(q * 8, 8), 8)
        return remote(dsnd.at[it + ITERS, rows], drecv.at[it, d - 1], send.at[5], dr.at[it, 1], dev)

    def den_all(it):
        return remote(drecv.at[it], drecv.at[it], send.at[5], dr.at[it, 1], sib)

    def tile(k):
        return slice(k * 128, (k + 1) * 128)

    def track_copy(it, k, d):
        qh, qz, dev = gpeer(d)
        rows = pl.ds(pl.multiple_of(qz * 8, 8), 8)
        return remote(
            gsnd.at[it, qh, rows, tile(k)], grecv.at[it, k, d - 1], send.at[6], wr.at[it, k], dev
        )

    def w_copy(it, k, d):
        ref = wth.at[it + 1, yh, rows_z, tile(k)]
        return remote(ref, ref, send.at[7], wr.at[it, 3], gpeer(d)[2])

    lane = lax.broadcasted_iota(jnp.int32, (8, 128), 1)
    lane64 = lax.broadcasted_iota(jnp.int32, (K, 128), 1)

    def mask_of(tb, b):
        return avail[tb, b].astype(F32)

    def ratio_of(b, h_low):
        recon = jnp.dot(wrow[...], h_low, preferred_element_type=F32)
        return (cbuf[:, half(b)].astype(F32) / recon).astype(BF16)

    def bins_half(it, j, which):
        b = 2 * j + which
        ratio = ratio_of(b, hbuf[it, j, :, half(which)].astype(BF16))
        left = jnp.concatenate(
            [wcol[:, tb * TB : (tb + 1) * TB] * mask_of(tb, b) for tb in range(NT)], axis=1
        ).astype(BF16)
        part[it, j, :, half(which)] = jnp.dot(left, ratio, preferred_element_type=F32)

    def tracks_half(it, j, which):
        b = 2 * j + which
        h_now = hbuf[it + 1, j, :, half(which)]
        h_low = h_now.astype(BF16)
        ratio = ratio_of(b, h_low)
        h_sum = jnp.sum(h_now, axis=1, keepdims=True)
        keep = jnp.zeros((8, 128), F32)
        for tb in range(NT):
            keep = jnp.where(lane == 64 + tb, mask_of(tb, b), keep)
        dacc[...] += h_sum * keep[0:1, :]
        term = lax.dot_general(h_low, ratio, (((1,), (1,)), ((), ())), preferred_element_type=F32)
        for tb in range(NT):
            s = slice(tb * TB, (tb + 1) * TB)
            acc[:, s] += term[:, s] * mask_of(tb, b)

    def spread_w(wt):
        wcol[...] = wt.astype(BF16).astype(F32)
        wrow[...] = wt.T.astype(BF16)

    w_copy_in.wait()
    avail_copy.wait()
    wt0 = wbuf[...]
    spread_w(wt0)
    wth[0, 0] = jnp.concatenate([wt0[:, :HALF], jnp.zeros((K, 64), F32)], axis=1)
    wth[0, 1] = pltpu.roll(wt0[:, 256:640], HALF, 1)

    def w_full(it):
        left = wth[it, 0]
        right = pltpu.roll(wth[it, 1], 64, 1)
        mid = jnp.where(lane64 < 64, left[:, 256:384], right[:, 0:128])
        return jnp.concatenate([left[:, 0:256], mid, right[:, 128:384]], axis=1)

    def start_den(it):
        wt = w_full(it)
        den = jnp.zeros((K, 128), F32)
        for tb in range(NT):
            row = jnp.zeros((8, 128), F32)
            for b in range(NB):
                row = jnp.where(lane == b, mask_of(tb, b), row)
            w_sum = jnp.sum(wt[:, tb * TB : (tb + 1) * TB], axis=1, keepdims=True)
            den = den + w_sum * row[0:1, :]
        dsnd[it] = den
        den_core(it).start()

    def stage_b(it, j):
        core_copy(it, j).wait_recv()
        part[it, j, :, half(c)] = part[it, j, :, half(c)] + crecv[it, j]
        for d in NEAR:
            reduce_copy(it, j, d).start()

        @pl.when(j == 0)
        def _():
            den_core(it).wait_recv()
            dsnd[it + ITERS] = dsnd[it] + dcrecv[it]
            for d in range(1, 8):
                den_copy(it, d).start()

    def stage_c(it, j):
        @pl.when(j == 0)
        def _():
            den_all(it).wait_recv()
            tot = dsnd[it + ITERS, rows_p]
            for d in range(1, 8):
                tot = tot + drecv[it, d - 1]
            dtot[...] = tot

        reduce_all(it, j).wait_recv()
        tot = part[it, j, rows_p, half(c)]
        for d in range(1, 8):
            tot = tot + rrecv[it, j, d - 1]
        den = jnp.sum(jnp.where(lane == 2 * j + c, dtot[...], 0.0), axis=1, keepdims=True)
        hbuf[it + 1, j, rows_p, half(c)] = hbuf[it, j, rows_p, half(c)] * tot / den
        for d in NEAR:
            gather_copy(it, j, d).start()

    def stage_d(it, j):
        gather_all(it, j).wait_recv()
        forward_copy(it, j, c).start()
        tracks_half(it, j, c)

    def stage_e(it, j):
        forward_copy(it, j, 1 - c).wait_recv()
        tracks_half(it, j, 1 - c)

        @pl.when(it == ITERS - 1)
        def _():
            out_copy(j).start()

    def pack_tracks(it):
        full = acc[...]
        dvec = dacc[...]
        gsnd[it, 0, :, 0:256] = full[:, 0:256]
        gsnd[it, 0, :, 256:384] = jnp.where(lane64 < 64, full[:, 256:384], dvec)
        right = pltpu.roll(full[:, 256:640], HALF, 1)
        gsnd[it, 1, :, 0:256] = right[:, 0:256]
        gsnd[it, 1, :, 256:384] = jnp.where(lane64 < 64, right[:, 256:384], dvec)

    def send_tracks(it):
        for k in TILES:
            for d in FAR:
                track_copy(it, k, d).start()

    def wait_tracks(it, k):
        remote(grecv.at[it, k], grecv.at[it, k], send.at[6], wr.at[it, k], sib).wait_recv()

    def update_w(it):
        divisor = None
        for k in TILES:
            wait_tracks(it, k)
            tot = gsnd[it, yh, rows_z, tile(k)]
            for d in range(1, 16):
                tot = tot + grecv[it, k, d - 1]
            if divisor is None:
                divisor = [tot[:, 64 + tb : 65 + tb] for tb in range(NT)]
            block = (lane + (yh * HALF + k * 128)) // TB
            den = jnp.ones((8, 128), F32)
            for tb in range(NT):
                den = jnp.where(block == tb, divisor[tb], den)
            wth[it + 1, yh, rows_z, tile(k)] = wth[it, yh, rows_z, tile(k)] * tot / den
            for d in FAR:
                w_copy(it, k, d).start()

    def wait_w(it):
        remote(grecv.at[it], grecv.at[it], send.at[7], wr.at[it, 3], sib).wait_recv()

    def iteration(it, _):
        acc[...] = jnp.zeros((K, ROWS), F32)
        dacc[...] = jnp.zeros((K, 128), F32)

        def first(j, _):
            @pl.when(it == 0)
            def _():
                h_copy(j).wait()
                count_copy(j).wait()

            @pl.when((it == 0) & (j == 0))
            def _():
                lax.fori_loop(1, NC, start_in, 0)

            bins_half(it, j, 1 - c)

            @pl.when((it == 0) & (j == 0))
            def _():
                pl.semaphore_wait(bar, 23)

            core_copy(it, j).start()

            @pl.when(j == 0)
            def _():
                start_den(it)

            @pl.when(j > 0)
            def _():
                stage_b(it, j - 1)

            bins_half(it, j, c)
            return 0

        lax.fori_loop(0, NC, first, 0)
        stage_b(it, NC - 1)

        def second(k, _):
            @pl.when(k < NC)
            def _():
                stage_c(it, k)

            @pl.when((k >= LAG) & (k < NC + LAG))
            def _():
                stage_d(it, k - LAG)

            @pl.when(k > LAG)
            def _():
                stage_e(it, k - LAG - 1)

            return 0

        lax.fori_loop(0, NC + LAG + 1, second, 0)
        pack_tracks(it)
        send_tracks(it)
        update_w(it)
        wait_w(it)
        wt = w_full(it + 1)

        @pl.when(it < ITERS - 1)
        def _():
            spread_w(wt)

        wbuf[...] = wt
        return 0

    lax.fori_loop(0, ITERS, iteration, 0)
    w_copy_out.start()

    def finish(j, _):
        out_copy(j).wait()
        return 0

    lax.fori_loop(0, NC, finish, 0)

    def sent(ref, s):
        remote(ref, ref, send.at[s], dr.at[0, 0], sib).wait_send()

    sent(crecv, 0)
    sent(rrecv, 1)
    sent(rrecv, 2)
    sent(crecv, 3)
    sent(dcrecv, 4)
    sent(drecv, 5)
    sent(grecv, 6)
    sent(grecv, 7)
    w_copy_out.wait()


def settle(w_ref, h_ref, w_out, h_out, sem):
    copies = [pltpu.make_async_copy(w_ref, w_out, sem.at[NC])]
    for j in range(NC):
        span = slice(j * CB, (j + 1) * CB)
        copies.append(pltpu.make_async_copy(h_ref.at[:, span], h_out.at[:, span], sem.at[j]))
    for copy in copies:
        copy.start()
    for copy in copies:
        copy.wait()


def body(counts, avail, track_factors, bin_factors):
    dma = pltpu.SemaphoreType.DMA
    vmem = pltpu.VMEM
    w_new, h_new = pl.pallas_call(
        kernel,
        name="factorize",
        out_shape=(
            pltpu.VMEM((K, ROWS), F32),
            pltpu.VMEM((K, COLS), F32),
        ),
        in_specs=[
            pl.BlockSpec(memory_space=pl.ANY),
            pl.BlockSpec(memory_space=pl.ANY),
            pl.BlockSpec(memory_space=pl.ANY),
            pl.BlockSpec(memory_space=pl.ANY),
        ],
        out_specs=(
            pl.BlockSpec(memory_space=pltpu.VMEM),
            pl.BlockSpec(memory_space=pltpu.VMEM),
        ),
        scratch_shapes=[
            pltpu.SMEM((NT, NB), jnp.int32),
            vmem((K, ROWS), F32),
            vmem((ROWS, COLS), BF16),
            vmem((ITERS + 1, NC, K, CB), F32),
            vmem((ITERS + 1, 2, K, WIDE), F32),
            vmem((ROWS, K), BF16),
            vmem((K, ROWS), F32),
            vmem((ITERS, NC, K, CB), F32),
            vmem((ITERS, NC, K, BB), F32),
            vmem((ITERS, NC, 7, 8, BB), F32),
            vmem((2 * ITERS, K, 128), F32),
            vmem((ITERS, K, 128), F32),
            vmem((ITERS, 7, 8, 128), F32),
            vmem((8, 128), F32),
            vmem((K, ROWS), F32),
            vmem((K, 128), F32),
            vmem((ITERS, 2, K, WIDE), F32),
            vmem((ITERS, 3, 15, 8, 128), F32),
            dma((NC,)),
            dma((NC,)),
            dma((NC,)),
            dma((3,)),
            dma((8,)),
            dma((ITERS, NC)),
            dma((ITERS, NC)),
            dma((ITERS, NC)),
            dma((ITERS, NC)),
            dma((ITERS, 2)),
            dma((ITERS, 4)),
        ],
        compiler_params=pltpu.CompilerParams(
            collective_id=0, has_side_effects=True, vmem_limit_bytes=56 * 1024 * 1024
        ),
    )(counts, avail, track_factors.T, bin_factors)
    anywhere = pl.BlockSpec(memory_space=pl.ANY)
    w_new, h_new = pl.pallas_call(
        settle,
        name="settle",
        out_shape=(jax.ShapeDtypeStruct((K, ROWS), F32), jax.ShapeDtypeStruct((K, COLS), F32)),
        in_specs=[anywhere, anywhere],
        out_specs=(anywhere, anywhere),
        scratch_shapes=[dma((NC + 1,))],
    )(*(pltpu.with_memory_space_constraint(v, pltpu.VMEM) for v in (w_new, h_new)))
    return w_new.T, h_new


def solution(mesh):
    placed = (P("track", "genome"), P("track", "genome"), P("track", None), P(None, "genome"))
    return jax.shard_map(
        body,
        mesh=mesh,
        in_specs=placed,
        out_specs=(P("track", None), P(None, "genome")),
        check_vma=False,
    )
```

time: 623 us -> 88.9 us (0.14)
  waiting for transfers between devices: 404 us -> 0 us
  blocking collectives: 135 us -> 0 us
  Pallas kernels: 0 us -> 88.1 us
  matrix products: 40.8 us -> 0 us
  local copies, waits for them, and re-layouts: 17.9 us -> 0 us
  between operations: 14 us -> 0.64 us
  other arithmetic: 10.5 us -> 0 us
    psum x4 -> x0, waiting for transfers between devices: 404 us -> none  [the longest x2 213 us: body(): num_tracks, den_tracks = lax.psum((num_rows, den_rows), 'genome')]
    psum x4 -> x0, blocking collectives: 135 us -> none  [the longest x2 84.5 us: body(): num_tracks, den_tracks = lax.psum((num_rows, den_rows), 'genome')]
    pallas_call x0 -> x2, Pallas kernels: none -> 88.1 us  [the longest x1 86.9 us: body(): pl.pallas_call(kernel, name='factorize', out_shape=(pltpu.VMEM((K, ROWS),...]
    dot_general x8 -> x0, matrix products: 40.8 us -> none  [the longest x2 20.3 us: body(): lax.dot_general(ratio, h_low, (((1,), (1,)), ((), ())), preferred_element...]
    unnamed x17 -> x0, local copies, waits for them, and re-layouts: 11.8 us -> none
    div x4 -> x0, other arithmetic: 7.47 us -> none  [the longest x2 4.87 us: body(): h_now = h_now * num_bins / den_full]
  transfers between devices with their start and end apart: 4 -> 0, of which waited for: 4 -> 0; matrix products, arithmetic and copies ran while one was open for 1% -> 0% of each run, Pallas kernels for 0% -> 0%
where the time goes in v2:
time: 88.9 us; the launch traced here: 88.7 us
  Pallas kernels  88.1 us (99%)
    pallas_call x1, Pallas kernels, body(): pl.pallas_call(kernel, name='factorize', out_shape=(pltpu.VMEM((K, ROWS),...  86.9 us

profile of v2, /device:TPU:2, one launch (start us, length us, event | category | flops | bytes accessed | tf_op | source)
XLA Modules:
  0.0 88.7 jit_solution(10823905777631994791)
XLA Ops:
  0.6 86.9 %factorize.1 = (f32[64,640]{1,0:T(8,128)S(1)}, f32[64,6144]{1,0:T(8,128)S(1)}) custom-call(bf16[640,6144]{1,0:T(8,128)(2,1)} %counts.1, s32[5,12]{1,0:T(8,128)} %avail_in.1, f32[64,640]{1,0:T(8,128)} %bitcast.2, f32[64,6144]{1,0:T(8,128)} %h_in.1), custom_call_target="tpu_custom_call" | custom-call | tf_op jit(solution)/shard_map/factorize/pallas_call | solution.py:384
  87.5 1.2 %settle.1 = (f32[64,640]{1,0:T(8,128)}, f32[64,6144]{1,0:T(8,128)}) custom-call(f32[64,640]{1,0:T(8,128)S(1)} %get-tuple-element.6.w_ref, f32[64,6144]{1,0:T(8,128)S(1)} %get-tuple-element.7.h_ref), custom_call_target="tpu_custom_call" | custom-call | tf_op jit(solution)/shard_map/settle/pallas_call | solution.py:437

commit v3 on v2

--- a/solution.py
+++ b/solution.py
@@ -19,7 +19,8 @@
 LAG = 6
 FAR = (12, 11, 13, 4, 10, 14, 3, 5, 9, 15, 2, 6, 8, 1, 7)
 NEAR = (6, 2, 5, 1, 7, 3, 4)
-TILES = (2, 0, 1)
+PIECES = 1
+SPANS = ((256, 128), (0, 256))
 CB = 2 * BB
 MESH = pl.DeviceIdType.MESH
 F32 = jnp.float32
@@ -67,12 +68,24 @@
         count_copy(j).start()
         return 0
 
+    def first_in(which):
+        rows = ROWS // PIECES
+        return [
+            pltpu.make_async_copy(
+                counts.at[r * rows : (r + 1) * rows, half(which)],
+                cbuf.at[r * rows : (r + 1) * rows, half(which)],
+                csem.at[which * NC],
+            )
+            for r in range(PIECES)
+        ]
+
     w_copy_in = pltpu.make_async_copy(w_in, wbuf, wsem.at[0])
-    w_copy_out = pltpu.make_async_copy(wbuf, w_out, wsem.at[1])
     w_copy_in.start()
-    avail_copy = pltpu.make_async_copy(avail_in, avail, wsem.at[2])
+    avail_copy = pltpu.make_async_copy(avail_in, avail, wsem.at[1])
     avail_copy.start()
-    start_in(0, 0)
+    h_copy(0).start()
+    for copy in first_in(1 - c) + first_in(c):
+        copy.start()
 
     bar = pltpu.get_barrier_semaphore()
     for d in FAR:
@@ -122,18 +135,17 @@
     def den_all(it):
         return remote(drecv.at[it], drecv.at[it], send.at[5], dr.at[it, 1], sib)
 
-    def tile(k):
-        return slice(k * 128, (k + 1) * 128)
-
     def track_copy(it, k, d):
         qh, qz, dev = gpeer(d)
         rows = pl.ds(pl.multiple_of(qz * 8, 8), 8)
+        lo, n = SPANS[k]
         return remote(
-            gsnd.at[it, qh, rows, tile(k)], grecv.at[it, k, d - 1], send.at[6], wr.at[it, k], dev
+            gsnd.at[it, qh, rows, lo : lo + n], grecv.at[it, d - 1, :, lo : lo + n], send.at[6], wr.at[it, k], dev
         )
 
     def w_copy(it, k, d):
-        ref = wth.at[it + 1, yh, rows_z, tile(k)]
+        lo, n = SPANS[k]
+        ref = wth.at[it + 1, yh, rows_z, lo : lo + n]
         return remote(ref, ref, send.at[7], wr.at[it, 3], gpeer(d)[2])
 
     lane = lax.broadcasted_iota(jnp.int32, (8, 128), 1)
@@ -252,27 +264,29 @@
         gsnd[it, 1, :, 256:384] = jnp.where(lane64 < 64, right[:, 256:384], dvec)
 
     def send_tracks(it):
-        for k in TILES:
+        for k in range(len(SPANS)):
             for d in FAR:
                 track_copy(it, k, d).start()
 
     def wait_tracks(it, k):
-        remote(grecv.at[it, k], grecv.at[it, k], send.at[6], wr.at[it, k], sib).wait_recv()
+        lo, n = SPANS[k]
+        ref = grecv.at[it, :, :, lo : lo + n]
+        remote(ref, ref, send.at[6], wr.at[it, k], sib).wait_recv()
 
     def update_w(it):
         divisor = None
-        for k in TILES:
+        for k, (lo, n) in enumerate(SPANS):
             wait_tracks(it, k)
-            tot = gsnd[it, yh, rows_z, tile(k)]
+            tot = gsnd[it, yh, rows_z, lo : lo + n]
             for d in range(1, 16):
-                tot = tot + grecv[it, k, d - 1]
+                tot = tot + grecv[it, d - 1, :, lo : lo + n]
             if divisor is None:
-                divisor = [tot[:, 64 + tb : 65 + tb] for tb in range(NT)]
-            block = (lane + (yh * HALF + k * 128)) // TB
-            den = jnp.ones((8, 128), F32)
+                divisor = [tot[:, n - 64 + tb : n - 63 + tb] for tb in range(NT)]
+            block = (lax.broadcasted_iota(jnp.int32, (8, n), 1) + (yh * HALF + lo)) // TB
+            den = jnp.ones((8, n), F32)
             for tb in range(NT):
                 den = jnp.where(block == tb, divisor[tb], den)
-            wth[it + 1, yh, rows_z, tile(k)] = wth[it, yh, rows_z, tile(k)] * tot / den
+            wth[it + 1, yh, rows_z, lo : lo + n] = wth[it, yh, rows_z, lo : lo + n] * tot / den
             for d in FAR:
                 w_copy(it, k, d).start()
 
@@ -287,27 +301,37 @@
             @pl.when(it == 0)
             def _():
                 h_copy(j).wait()
-                count_copy(j).wait()
+
+                @pl.when(j == 0)
+                def _():
+                    pltpu.make_async_copy(
+                        counts.at[:, half(1 - c)], cbuf.at[:, half(1 - c)], csem.at[(1 - c) * NC]
+                    ).wait()
+
+                @pl.when(j > 0)
+                def _():
+                    count_copy(j).wait()
+
+            bins_half(it, j, 1 - c)
 
             @pl.when((it == 0) & (j == 0))
             def _():
+                pl.semaphore_wait(bar, 23)
+
+            core_copy(it, j).start()
+
+            @pl.when(j == 0)
+            def _():
+                start_den(it)
+
+            @pl.when(j > 0)
+            def _():
+                stage_b(it, j - 1)
+
+            @pl.when((it == 0) & (j == 0))
+            def _():
+                pltpu.make_async_copy(counts.at[:, half(c)], cbuf.at[:, half(c)], csem.at[c * NC]).wait()
                 lax.fori_loop(1, NC, start_in, 0)
-
-            bins_half(it, j, 1 - c)
-
-            @pl.when((it == 0) & (j == 0))
-            def _():
-                pl.semaphore_wait(bar, 23)
-
-            core_copy(it, j).start()
-
-            @pl.when(j == 0)
-            def _():
-                start_den(it)
-
-            @pl.when(j > 0)
-            def _():
-                stage_b(it, j - 1)
 
             bins_half(it, j, c)
             return 0
@@ -341,11 +365,10 @@
         def _():
             spread_w(wt)
 
-        wbuf[...] = wt
+        w_out[...] = wt
         return 0
 
     lax.fori_loop(0, ITERS, iteration, 0)
-    w_copy_out.start()
 
     def finish(j, _):
         out_copy(j).wait()
@@ -364,7 +387,6 @@
     sent(drecv, 5)
     sent(grecv, 6)
     sent(grecv, 7)
-    w_copy_out.wait()
 
 
 def settle(w_ref, h_ref, w_out, h_out, sem):
@@ -416,11 +438,11 @@
             vmem((K, ROWS), F32),
             vmem((K, 128), F32),
             vmem((ITERS, 2, K, WIDE), F32),
-            vmem((ITERS, 3, 15, 8, 128), F32),
+            vmem((ITERS, 15, 8, WIDE), F32),
+            dma((NC + 1,)),
             dma((NC,)),
             dma((NC,)),
-            dma((NC,)),
-            dma((3,)),
+            dma((2,)),
             dma((8,)),
             dma((ITERS, NC)),
             dma((ITERS, NC)),

time: 88.9 us -> 87.9 us (0.989)
  Pallas kernels: 88.1 us -> 87.1 us
    pallas_call x1, Pallas kernels: 86.9 us -> 85.8 us  [body(): pl.pallas_call(kernel, name='factorize', out_shape=(pltpu.VMEM((K, ROWS),...]
where the time goes in v3:
time: 87.9 us; the launch traced here: 87.7 us
  Pallas kernels  87.1 us (99%)
    pallas_call x1, Pallas kernels, body(): pl.pallas_call(kernel, name='factorize', out_shape=(pltpu.VMEM((K, ROWS),...  85.8 us

profile of v3, /device:TPU:2, one launch (start us, length us, event | category | flops | bytes accessed | tf_op | source)
XLA Modules:
  0.0 87.7 jit_solution(8481026536385687774)
XLA Ops:
  0.6 85.8 %factorize.1 = (f32[64,640]{1,0:T(8,128)S(1)}, f32[64,6144]{1,0:T(8,128)S(1)}) custom-call(bf16[640,6144]{1,0:T(8,128)(2,1)} %counts.1, s32[5,12]{1,0:T(8,128)} %avail_in.1, f32[64,640]{1,0:T(8,128)} %bitcast.2, f32[64,6144]{1,0:T(8,128)} %h_in.1), custom_call_target="tpu_custom_call" | custom-call | tf_op jit(solution)/shard_map/factorize/pallas_call | solution.py:406
  86.5 1.2 %settle.1 = (f32[64,640]{1,0:T(8,128)}, f32[64,6144]{1,0:T(8,128)}) custom-call(f32[64,640]{1,0:T(8,128)S(1)} %get-tuple-element.6.w_ref, f32[64,6144]{1,0:T(8,128)S(1)} %get-tuple-element.7.h_ref), custom_call_target="tpu_custom_call" | custom-call | tf_op jit(solution)/shard_map/settle/pallas_call | solution.py:459

commit v4 on v3

--- a/solution.py
+++ b/solution.py
@@ -61,7 +61,7 @@
         return pltpu.make_async_copy(h_in.at[:, cols(j)], hbuf.at[0, j], hsem.at[j])
 
     def out_copy(j):
-        return pltpu.make_async_copy(hbuf.at[ITERS, j], h_out.at[:, cols(j)], osem.at[j])
+        return pltpu.make_async_copy(hbuf.at[ITERS, j], h_out.at[:, cols(j)], osem.at[0])
 
     def start_in(j, _):
         h_copy(j).start()
@@ -103,26 +103,26 @@
     rows_z = pl.ds(pl.multiple_of(z * 8, 8), 8)
 
     def core_copy(it, j):
-        return remote(part.at[it, j, :, half(1 - c)], crecv.at[it, j], send.at[0], cr.at[it, j], sib)
+        return remote(part.at[it, j, :, half(1 - c)], crecv.at[it, j], send.at[0], cr.at[j], sib)
 
     def reduce_copy(it, j, d):
         q, dev = tpeer(d)
         rows = pl.ds(pl.multiple_of(q * 8, 8), 8)
-        return remote(part.at[it, j, rows, half(c)], rrecv.at[it, j, d - 1], send.at[1], rr.at[it, j], dev)
+        return remote(part.at[it, j, rows, half(c)], rrecv.at[it, j, d - 1], send.at[1], rr.at[j], dev)
 
     def reduce_all(it, j):
-        return remote(rrecv.at[it, j], rrecv.at[it, j], send.at[1], rr.at[it, j], sib)
+        return remote(rrecv.at[it, j], rrecv.at[it, j], send.at[1], rr.at[j], sib)
 
     def gather_copy(it, j, d):
         ref = hbuf.at[it + 1, j, rows_p, half(c)]
-        return remote(ref, ref, send.at[2], gr.at[it, j], tpeer(d)[1])
+        return remote(ref, ref, send.at[2], gr.at[j], tpeer(d)[1])
 
     def gather_all(it, j):
-        return remote(rrecv.at[it, j], rrecv.at[it, j], send.at[2], gr.at[it, j], sib)
+        return remote(rrecv.at[it, j], rrecv.at[it, j], send.at[2], gr.at[j], sib)
 
     def forward_copy(it, j, which):
         ref = hbuf.at[it + 1, j, :, half(which)]
-        return remote(ref, ref, send.at[3], fr.at[it, j], sib)
+        return remote(ref, ref, send.at[3], fr.at[j], sib)
 
     def den_core(it):
         return remote(dsnd.at[it], dcrecv.at[it], send.at[4], dr.at[it, 0], sib)
@@ -307,6 +307,7 @@
                     pltpu.make_async_copy(
                         counts.at[:, half(1 - c)], cbuf.at[:, half(1 - c)], csem.at[(1 - c) * NC]
                     ).wait()
+                    lax.fori_loop(1, NC, start_in, 0)
 
                 @pl.when(j > 0)
                 def _():
@@ -331,7 +332,6 @@
             @pl.when((it == 0) & (j == 0))
             def _():
                 pltpu.make_async_copy(counts.at[:, half(c)], cbuf.at[:, half(c)], csem.at[c * NC]).wait()
-                lax.fori_loop(1, NC, start_in, 0)
 
             bins_half(it, j, c)
             return 0
@@ -370,11 +370,7 @@
 
     lax.fori_loop(0, ITERS, iteration, 0)
 
-    def finish(j, _):
-        out_copy(j).wait()
-        return 0
-
-    lax.fori_loop(0, NC, finish, 0)
+    pltpu.make_async_copy(hbuf.at[ITERS], hbuf.at[ITERS], osem.at[0]).wait()
 
     def sent(ref, s):
         remote(ref, ref, send.at[s], dr.at[0, 0], sib).wait_send()
@@ -441,13 +437,13 @@
             vmem((ITERS, 15, 8, WIDE), F32),
             dma((NC + 1,)),
             dma((NC,)),
-            dma((NC,)),
+            dma((1,)),
             dma((2,)),
             dma((8,)),
-            dma((ITERS, NC)),
-            dma((ITERS, NC)),
-            dma((ITERS, NC)),
-            dma((ITERS, NC)),
+            dma((NC,)),
+            dma((NC,)),
+            dma((NC,)),
+            dma((NC,)),
             dma((ITERS, 2)),
             dma((ITERS, 4)),
         ],

time: 87.9 us -> 87 us (0.990)
  Pallas kernels: 87.1 us -> 86.2 us
where the time goes in v4:
time: 87 us; the launch traced here: 86.9 us
  Pallas kernels  86.2 us (99%)
    pallas_call x1, Pallas kernels, body(): pl.pallas_call(kernel, name='factorize', out_shape=(pltpu.VMEM((K, ROWS),...  85 us

profile of v4, /device:TPU:2, one launch (start us, length us, event | category | flops | bytes accessed | tf_op | source)
XLA Modules:
  0.0 86.9 jit_solution(18124951309813353585)
XLA Ops:
  0.6 85.0 %factorize.1 = (f32[64,640]{1,0:T(8,128)S(1)}, f32[64,6144]{1,0:T(8,128)S(1)}) custom-call(bf16[640,6144]{1,0:T(8,128)(2,1)} %counts.1, s32[5,12]{1,0:T(8,128)} %avail_in.1, f32[64,640]{1,0:T(8,128)} %bitcast.2, f32[64,6144]{1,0:T(8,128)} %h_in.1), custom_call_target="tpu_custom_call" | custom-call | tf_op jit(solution)/shard_map/factorize/pallas_call | solution.py:402
  85.6 1.2 %settle.1 = (f32[64,640]{1,0:T(8,128)}, f32[64,6144]{1,0:T(8,128)}) custom-call(f32[64,640]{1,0:T(8,128)S(1)} %get-tuple-element.6.w_ref, f32[64,6144]{1,0:T(8,128)S(1)} %get-tuple-element.7.h_ref), custom_call_target="tpu_custom_call" | custom-call | tf_op jit(solution)/shard_map/settle/pallas_call | solution.py:455

commit v5 on v4

--- a/solution.py
+++ b/solution.py
@@ -125,28 +125,28 @@
         return remote(ref, ref, send.at[3], fr.at[j], sib)
 
     def den_core(it):
-        return remote(dsnd.at[it], dcrecv.at[it], send.at[4], dr.at[it, 0], sib)
+        return remote(dsnd.at[it], dcrecv.at[it], send.at[4], dr.at[0], sib)
 
     def den_copy(it, d):
         q, dev = tpeer(d)
         rows = pl.ds(pl.multiple_of(q * 8, 8), 8)
-        return remote(dsnd.at[it + ITERS, rows], drecv.at[it, d - 1], send.at[5], dr.at[it, 1], dev)
+        return remote(dsnd.at[it + ITERS, rows], drecv.at[it, d - 1], send.at[5], dr.at[1], dev)
 
     def den_all(it):
-        return remote(drecv.at[it], drecv.at[it], send.at[5], dr.at[it, 1], sib)
+        return remote(drecv.at[it], drecv.at[it], send.at[5], dr.at[1], sib)
 
     def track_copy(it, k, d):
         qh, qz, dev = gpeer(d)
         rows = pl.ds(pl.multiple_of(qz * 8, 8), 8)
         lo, n = SPANS[k]
         return remote(
-            gsnd.at[it, qh, rows, lo : lo + n], grecv.at[it, d - 1, :, lo : lo + n], send.at[6], wr.at[it, k], dev
+            gsnd.at[it, qh, rows, lo : lo + n], grecv.at[it, d - 1, :, lo : lo + n], send.at[6], wr.at[k], dev
         )
 
     def w_copy(it, k, d):
         lo, n = SPANS[k]
         ref = wth.at[it + 1, yh, rows_z, lo : lo + n]
-        return remote(ref, ref, send.at[7], wr.at[it, 3], gpeer(d)[2])
+        return remote(ref, ref, send.at[7], wr.at[2], gpeer(d)[2])
 
     lane = lax.broadcasted_iota(jnp.int32, (8, 128), 1)
     lane64 = lax.broadcasted_iota(jnp.int32, (K, 128), 1)
@@ -271,7 +271,7 @@
     def wait_tracks(it, k):
         lo, n = SPANS[k]
         ref = grecv.at[it, :, :, lo : lo + n]
-        remote(ref, ref, send.at[6], wr.at[it, k], sib).wait_recv()
+        remote(ref, ref, send.at[6], wr.at[k], sib).wait_recv()
 
     def update_w(it):
         divisor = None
@@ -291,7 +291,7 @@
                 w_copy(it, k, d).start()
 
     def wait_w(it):
-        remote(grecv.at[it], grecv.at[it], send.at[7], wr.at[it, 3], sib).wait_recv()
+        remote(grecv.at[it], grecv.at[it], send.at[7], wr.at[2], sib).wait_recv()
 
     def iteration(it, _):
         acc[...] = jnp.zeros((K, ROWS), F32)
@@ -337,10 +337,11 @@
             return 0
 
         lax.fori_loop(0, NC, first, 0)
+        stage_c(it, 0)
         stage_b(it, NC - 1)
 
         def second(k, _):
-            @pl.when(k < NC)
+            @pl.when((k > 0) & (k < NC))
             def _():
                 stage_c(it, k)
 
@@ -373,7 +374,7 @@
     pltpu.make_async_copy(hbuf.at[ITERS], hbuf.at[ITERS], osem.at[0]).wait()
 
     def sent(ref, s):
-        remote(ref, ref, send.at[s], dr.at[0, 0], sib).wait_send()
+        remote(ref, ref, send.at[s], dr.at[0], sib).wait_send()
 
     sent(crecv, 0)
     sent(rrecv, 1)
@@ -444,8 +445,8 @@
             dma((NC,)),
             dma((NC,)),
             dma((NC,)),
-            dma((ITERS, 2)),
-            dma((ITERS, 4)),
+            dma((2,)),
+            dma((3,)),
         ],
         compiler_params=pltpu.CompilerParams(
             collective_id=0, has_side_effects=True, vmem_limit_bytes=56 * 1024 * 1024

time: 87 us -> 86.9 us (level)
  no operation moved by 1% of the time
where the time goes in v5:
time: 86.9 us; the launch traced here: 86.7 us
  Pallas kernels  86 us (99%)
    pallas_call x1, Pallas kernels, body(): pl.pallas_call(kernel, name='factorize', out_shape=(pltpu.VMEM((K, ROWS),...  84.8 us

profile of v5, /device:TPU:2, one launch (start us, length us, event | category | flops | bytes accessed | tf_op | source)
XLA Modules:
  0.0 86.7 jit_solution(17406071377006932677)
XLA Ops:
  0.6 84.8 %factorize.1 = (f32[64,640]{1,0:T(8,128)S(1)}, f32[64,6144]{1,0:T(8,128)S(1)}) custom-call(bf16[640,6144]{1,0:T(8,128)(2,1)} %counts.1, s32[5,12]{1,0:T(8,128)} %avail_in.1, f32[64,640]{1,0:T(8,128)} %bitcast.2, f32[64,6144]{1,0:T(8,128)} %h_in.1), custom_call_target="tpu_custom_call" | custom-call | tf_op jit(solution)/shard_map/factorize/pallas_call | solution.py:403
  85.4 1.2 %settle.1 = (f32[64,640]{1,0:T(8,128)}, f32[64,6144]{1,0:T(8,128)}) custom-call(f32[64,640]{1,0:T(8,128)S(1)} %get-tuple-element.6.w_ref, f32[64,6144]{1,0:T(8,128)S(1)} %get-tuple-element.7.h_ref), custom_call_target="tpu_custom_call" | custom-call | tf_op jit(solution)/shard_map/settle/pallas_call | solution.py:456
